TPU v7x, 256 devices: a whole 4x4x8 slice. The times are simulated.
256 devices in a mesh: prow: 8 (over z), pcol: 32 (over x, y, core).
Axes of the slice: x: 4, y: 4, z: 8, core: 2. Of those that a mesh axis runs over, the one named last changes fastest.
Arguments:
- matrix: bfloat16 [6, 4096, 2, 16384], P(None, 'prow', None, 'pcol'), may hold values from -6 to 6
- diag_inverses: bfloat16 [512, 512], P('prow', 'pcol'), may hold values from -2 to 2, as said below
Outputs:
- updated: bfloat16 [6, 4096, 2, 16384], P(None, 'prow', None, 'pcol')
Inputs may be any that keep to these rules, and one draw needn't show every extreme that they name: `diag_inverses`: strictly below the diagonal: the off-diagonal part of the inverse of a unit lower factor; on and above: the inverse of an upper factor, whose diagonal entries have magnitudes between 1 / sqrt(512) and 2 / sqrt(512).
All inputs are finite; a program needn't handle non-finite values.
Results may differ from a plain program's by a relative error of at most 0.0055.
Values may be sent and summed in bfloat16 or wider, within the bound.
A program may use at most 64 MiB of HBM per device.

v0:
```python
import jax
import jax.numpy as jnp
from jax import lax
from jax.sharding import PartitionSpec as P


def broadcast(shard, axis, root):
    mine = lax.axis_index(axis) == root
    return lax.psum(jnp.where(mine, shard, jnp.zeros_like(shard)), axis)


def shards(matrix, diag_inverses):
    row_blocks, width, col_blocks, _ = matrix.shape
    local_rows = row_blocks * width
    local_cols = col_blocks * width
    partial_value = lax.all_gather(diag_inverses, "pcol", axis=1, tiled=True)
    packed = lax.all_gather(partial_value, "prow", axis=0, tiled=True)
    row_index = lax.broadcasted_iota(jnp.int32, (width, width), 0)
    col_index = lax.broadcasted_iota(jnp.int32, (width, width), 1)
    zero_bf = jnp.zeros((width, width), packed.dtype)
    one_bf = jnp.ones((width, width), packed.dtype)
    lower_inv = jnp.where(col_index < row_index, packed, zero_bf)
    lower_inv = jnp.where(col_index == row_index, one_bf, lower_inv)
    upper_inv = jnp.where(col_index >= row_index, packed, zero_bf)
    owner_row = lax.axis_index("prow") == 0
    owner_col = lax.axis_index("pcol") == 0
    grid = matrix.reshape(local_rows, local_cols)
    column_first = matrix[:, :, 0, :].reshape(local_rows, width)
    row_first = matrix[0].reshape(width, local_cols)
    l_solved = lax.cond(
        owner_col,
        lambda: jnp.dot(column_first, upper_inv, preferred_element_type=jnp.float32).astype(
            matrix.dtype
        ),
        lambda: jnp.zeros((local_rows, width), matrix.dtype),
    )
    l_panel = broadcast(l_solved, "pcol", 0)
    u_solved = lax.cond(
        owner_row,
        lambda: jnp.dot(lower_inv, row_first, preferred_element_type=jnp.float32).astype(
            matrix.dtype
        ),
        lambda: jnp.zeros((width, local_cols), matrix.dtype),
    )
    u_panel = broadcast(u_solved, "prow", 0)
    product = jnp.dot(l_panel, u_panel, preferred_element_type=jnp.float32)
    trailing = (grid.astype(jnp.float32) - product).astype(matrix.dtype)
    head_rows = jnp.where(owner_row, u_panel, trailing[:width])
    merged = jnp.concatenate([head_rows, trailing[width:]], axis=0)
    left_cols = jnp.where(owner_col, l_panel, merged[:, :width])
    corner = jnp.where(owner_row & owner_col, grid[:width, :width], left_cols[:width])
    left_cols = jnp.concatenate([corner, left_cols[width:]], axis=0)
    result = jnp.concatenate([left_cols, merged[:, width:]], axis=1)
    return result.reshape(matrix.shape)


def solution(mesh):
    in_specs = (P(None, "prow", None, "pcol"), P("prow", "pcol"))
    out_specs = P(None, "prow", None, "pcol")
    return jax.shard_map(shards, mesh=mesh, in_specs=in_specs, out_specs=out_specs, check_vma=False)
```

profile of v0, /device:TPU:96, one launch (start us, length us, event | category | flops | bytes accessed | tf_op | source)
XLA Modules:
  0.0 295.0 jit_solution(4127519766386287326)
XLA Ops:
  6.5 24.9 %all_gather.6 = bf16[64,512]{0,1:T(8,128)(2,1)S(1)} all-gather(bf16[64,16]{0,1:T(8,128)(2,1)} %param.7), channel_id=1, replica_groups=mesh['prow'=8,'pcol'=32] {'pcol'}, dimensions={1}, use_global_device_ids=true | all-gather | bytes 67584 | tf_op jit(solution)/shard_map/all_gather | solution.py:16
  31.5 26.2 %all_gather.7 = bf16[512,512]{1,0:T(8,128)(2,1)S(1)} all-gather(bf16[64,512]{1,0:T(8,128)(2,1)S(1)} %copy.12), channel_id=1, replica_groups=mesh['prow'=8,'pcol'=32] {'prow'}, dimensions={0}, use_global_device_ids=true | all-gather | bytes 589824 | tf_op jit(solution)/shard_map/all_gather | solution.py:17
  57.8 0.1 iota.20
  58.0 0.1 conditional.3
  58.0 0.1 broadcast.9
  58.1 1.1 broadcast_select_fusion.1
  59.5 11.4 %conditional.2 = (bf16[3072,512]{1,0:T(8,128)(2,1)S(1)}) conditional(s32[]{:T(128)} %convert_element_type.22, () %tuple.21, (s32[512,512]{1,0:T(8,128)S(1)}, s32[512,512]{1,0:T(8,128)S(1)}, bf16[512,512]{1,0:T(8,128)(2,1)S(1)}, bf16[512,512]{1,0:T(8,128)(2,1)S(1)}, bf16[6,512,2,512]{3,2,1,0:T(2,128)(2,1)}) %tuple.22), branch_computations={%region_0.1_spmd, %region_1.2_spmd} | conditional | flops 1612709888 | bytes 34603016 | solution.py:30
  59.5 3.9 %copy.13 = bf16[6,512,2,512]{3,1,0,2:T(8,128)(2,1)S(1)} copy(bf16[6,512,2,512]{3,2,1,0:T(2,128)(2,1)} %get-tuple-element.93) | data formatting | bytes 12582912 | tf_op jit(solution)/shard_map
  63.5 0.4 slice.37
  63.9 3.7 %fusion = bf16[3072,512]{0,1:T(8,128)(2,1)} fusion(bf16[3072,512]{1,0:T(8,128)(2,1)S(1)} %bitcast.18, bf16[512,512]{1,0:T(8,128)(2,1)S(1)} %get-tuple-element.62, bf16[512,512]{1,0:T(8,128)(2,1)S(1)} %get-tuple-element.63, s32[512,512]{1,0:T(8,128)S(1)} %get-tuple-element.60, s32[512,512]{1,0:T(8,128)S(1)} %get-tuple-element.61), kind=kOutput, calls=%fused_computation.1 | convolution fusion | flops 1612709888 | bytes 9437184 | tf_op jit(solution)/shard_map/cond/branch_1_fun/dot_general | solution.py:32
  67.5 3.2 %copy.16 = bf16[3072,512]{1,0:T(8,128)(2,1)S(1)} copy(bf16[3072,512]{0,1:T(8,128)(2,1)} %fusion) | data formatting | bytes 6291456 | tf_op jit(solution)/shard_map/cond | solution.py:30
  70.9 1.9 broadcast_select_fusion
  72.8 7.6 %copy.18 = bf16[384,8,2,512]{3,1,2,0:T(8,128)(2,1)} copy(bf16[384,8,2,512]{3,2,1,0:T(2,128)(2,1)} %bitcast.13) | data formatting | bytes 12582912
  80.4 52.6 %all-reduce.5.cloned.1.call-done = bf16[512,1024]{1,0:T(8,128)(2,1)} async-done(((bf16[512,1024]{1,0:T(8,128)(2,1)}), bf16[512,1024]{1,0:T(8,128)(2,1)}) %all-reduce.5.cloned.1.call-update) | async-done | bytes 1048592 | tf_op jit(solution)/shard_map/psum | solution.py:9
  133.0 122.6 %all-reduce.3.cloned.1.call-done = bf16[3072,512]{1,0:T(8,128)(2,1)} async-done(((bf16[3072,512]{1,0:T(8,128)(2,1)}), bf16[3072,512]{1,0:T(8,128)(2,1)}) %all-reduce.3.cloned.1.call-update) | async-done | bytes 3145744 | tf_op jit(solution)/shard_map/psum | solution.py:9
  255.6 7.5 %subtract_convert_fusion = bf16[3072,1024]{1,0:T(8,128)(2,1)S(1)} fusion(bf16[3072,1024]{1,0:T(8,128)(2,1)} %bitcast.14, bf16[3072,512]{1,0:T(8,128)(2,1)} %all-reduce.3.cloned.1.call-done, bf16[512,1024]{1,0:T(8,128)(2,1)} %all-reduce.5.cloned.1.call-done), kind=kOutput, calls=%fused_computation.11 | convolution fusion | flops 3230662656 | bytes 16777216 | tf_op jit(solution)/shard_map/dot_general | solution.py:46
  263.1 0.6 slice.40
  263.7 0.6 copy-done.1
  264.4 0.9 copy-done
  265.3 1.4 fusion.8
  266.7 0.2 slice.44
  266.8 1.1 slice_select_fusion.1
  268.0 9.1 %fusion.6 = bf16[3072,1024]{1,0:T(8,128)(2,1)} fusion(bf16[512,1024]{1,0:T(8,128)(2,1)S(1)} %slice_select_fusion, bf16[2560,512]{1,0:T(8,128)(2,1)S(1)} %slice.44, bf16[512,512]{1,0:T(8,128)(2,1)S(1)} %slice_select_fusion.1, bf16[2560,1024]{1,0:T(8,128)(2,1)S(1)} %slice.40), kind=kLoop, calls=%fused_computation.14 | loop fusion | flops 34603008 | bytes 15728640 | tf_op jit(solution)/shard_map/concatenate | solution.py:53
  277.1 11.1 %reshape.7 = bf16[6,512,2,512]{3,2,1,0:T(2,128)(2,1)} reshape(bf16[3072,1024]{1,0:T(8,128)(2,1)} %fusion.6) | data formatting | bytes 12582912 | tf_op jit(solution)/shard_map/reshape | solution.py:54
  (12 shorter events, 0.6 us)
Async XLA Ops:
  6.5 126.4 %all-reduce.5.cloned.1.call-start = ((), (), s32[]{:S(2)}) async-start(), calls=%async_computation.1 | async-start | bytes 2097152 | tf_op jit(solution)/shard_map/psum | solution.py:9
  59.3 196.3 %all-reduce.3.cloned.1.call-start = ((), (), s32[]{:S(2)}) async-start(), calls=%async_computation | async-start | bytes 6291456 | tf_op jit(solution)/shard_map/psum | solution.py:9
  263.1 1.2 copy-start.1
  263.1 2.2 copy-start
Sparse Core Ops, SparseCore 0:
  59.4 73.5 all-reduce.4
  136.3 119.2 all-reduce.2
where the time goes:
time: 297 us; the launch traced here: 295 us
  waiting for transfers between devices  175 us (59%)
  blocking collectives  51.1 us (17%)
  local copies, waits for them, and re-layouts  29.1 us (10%)
  other arithmetic  14.7 us (5%)
  between operations  13.5 us (5%)
  matrix products  11.2 us (4%)
    psum x2, waiting for transfers between devices, broadcast(): return lax.psum(jnp.where(mine, shard, jnp.zeros_like(shard)), axis)  175 us
    all_gather x1, blocking collectives, shards(): packed = lax.all_gather(partial_value, 'prow', axis=0, tiled=True)  26.2 us
    all_gather x1, blocking collectives, shards(): partial_value = lax.all_gather(diag_inverses, 'pcol', axis=1, tiled=True)  24.9 us
    reshape x1, local copies, waits for them, and re-layouts, shards(): return result.reshape(matrix.shape)  11.1 us
    concatenate x1, other arithmetic, shards(): result = jnp.concatenate([left_cols, merged[:, width:]], axis=1)  9.1 us
    unnamed x5, local copies, waits for them, and re-layouts  9.08 us
    dot_general x1, matrix products, shards(): product = jnp.dot(l_panel, u_panel, preferred_element_type=jnp.float32)  7.5 us
  transfers between devices with their start and end apart: 2, of which 2 were waited for; matrix products, arithmetic and copies ran while one was open for 7% of the time, Pallas kernels for 0%

commit v1 on v0

v1 whole, which is shorter than its diff:
```python
import jax
import jax.numpy as jnp
from jax import lax
from jax.experimental import pallas as pl
from jax.experimental.pallas import tpu as pltpu
from jax.sharding import PartitionSpec as P

MESH = pl.DeviceIdType.MESH
BF16, F32 = jnp.bfloat16, jnp.float32
NB = 512
ROWS = 6 * NB
NZ = 8
STEPS = 16
LCH = ROWS // (4 * STEPS)
UCH = 64
BLK = 256


def parent(tree, node):
    bit = 1 << tree
    if not node & bit:
        return node | bit
    if node == bit:
        return 0
    for step in range(1, 4):
        other = 1 << ((tree + step) % 4)
        if node & other:
            return node ^ other


def depth(tree, node):
    return 0 if node == 0 else 1 + depth(tree, parent(tree, node))


def table(bits):
    return sum(1 << node for node in range(16) if bits(node))


CHILD = [[table(lambda v: v ^ (1 << j) and parent(i, v ^ (1 << j)) == v) for j in range(4)] for i in range(4)]
DEPTH = [[table(lambda v: (depth(i, v) >> b) & 1) for b in range(3)] for i in range(4)]


def gray_position(code):
    return code ^ (code >> 1)


def block_column(block):
    core, node = divmod(block, 16)
    return gray_position(node % 4) * 8 + gray_position(node // 4) * 2 + core


def kernel(a_hbm, d_ref, out_ref, av, sf, lraw, uraw, ub, uinv, linv, dz, dt, dtf,
           a_sem, l_send, l_recv, s_send, u_send, u_recv, z_send, z_recv, d_send, d_recv):
    z = lax.axis_index("prow")
    col = lax.axis_index("pcol")
    core = col % 2
    gx, gy = col // 8, (col // 2) % 4
    gx = gx ^ (gx >> 1)
    gy = gy ^ (gy >> 1)
    node = gx + 4 * gy
    sibling = col + 1 - 2 * core
    source = col == 0

    def near(dim):
        px, py = (gx ^ (1 << dim), gy) if dim < 2 else (gx, gy ^ (1 << (dim - 2)))
        return (px ^ (px >> 1)) * 8 + (py ^ (py >> 1)) * 2 + core

    nears = [near(dim) for dim in range(4)]

    def look(first, second):
        return (jnp.where(core == 0, first, second) >> node) & 1

    def load_a(piece):
        rows = pl.ds(pl.multiple_of(piece * (NB * 8), NB * 8), NB * 8)
        return pltpu.make_async_copy(a_hbm.at[rows], av.at[rows], a_sem.at[piece])

    for piece in range(6):
        load_a(piece).start()

    barrier = pltpu.get_barrier_semaphore()
    for step in range(1, NZ):
        pl.semaphore_signal(barrier, inc=1, device_id=((z + step) % NZ, col), device_id_type=MESH)
    for other in nears + [sibling]:
        pl.semaphore_signal(barrier, inc=1, device_id=(z, other), device_id_type=MESH)
    pl.semaphore_wait(barrier, NZ + 4)

    def z_copy(step):
        return pltpu.make_async_remote_copy(
            src_ref=d_ref, dst_ref=dz.at[z], send_sem=z_send.at[step - 1], recv_sem=z_recv.at[step - 1],
            device_id=((z + step) % NZ, col), device_id_type=MESH)

    for step in range(1, NZ):
        z_copy(step).start()
    dz[z] = d_ref[...]

    def d_copy(dim):
        if dim < 4:
            base = core * 16 + (node // (1 << dim)) * (1 << dim)
            blocks, target = pl.ds(base, 1 << dim), nears[dim]
        else:
            blocks, target = pl.ds(core * 16, 16), sibling
        return pltpu.make_async_remote_copy(
            src_ref=dt.at[blocks], dst_ref=dt.at[blocks], send_sem=d_send.at[dim], recv_sem=d_recv.at[dim],
            device_id=(z, target), device_id_type=MESH)

    def u_chunk(way, chunk):
        rows = pl.ds(pl.multiple_of((chunk % 8) * UCH, UCH), UCH)
        return uraw.at[2 * way + chunk // 8, rows]

    def u_copy(way, chunk):
        target = (z + 1) % NZ if way == 0 else (z + NZ - 1) % NZ
        part = u_chunk(way, chunk)
        return pltpu.make_async_remote_copy(
            src_ref=part, dst_ref=part, send_sem=u_send.at[way], recv_sem=u_recv.at[way, chunk],
            device_id=(target, col), device_id_type=MESH)

    def l_chunk(tree, chunk):
        return lraw.at[pl.ds(pl.multiple_of((chunk * 4 + tree) * LCH, LCH), LCH)]

    def l_copy(tree, chunk, target, sem):
        part = l_chunk(tree, chunk)
        return pltpu.make_async_remote_copy(
            src_ref=part, dst_ref=part, send_sem=sem, recv_sem=l_recv.at[tree, chunk],
            device_id=(z, target), device_id_type=MESH)

    def spread(first, rows):
        first = pl.multiple_of(first * 8, 16)
        sf[pl.ds(0, rows * 8), :] = av[pl.ds(first, rows * 8), :].astype(F32)

    hop_plus, hop_minus = z, (NZ - z) % NZ
    own, sends, hops = [], [], []
    for k in range(2):
        own.append(2 * core + k)
        sends.append([look(CHILD[k][dim], CHILD[2 + k][dim]) == 1 for dim in range(4)])
        hops.append(sum(look(DEPTH[k][b], DEPTH[2 + k][b]) << b for b in range(3)) + core)
    others, other_hops = [], []
    for k in range(2):
        tree = 2 * (1 - core) + k
        hop = sum(((jnp.where(core == 0, DEPTH[2 + k][b], DEPTH[k][b]) >> node) & 1) << b for b in range(3))
        others.append(tree)
        other_hops.append(jnp.where(source, 0, hop + (1 - core) + 1))
    root_second = (node == 0) & (core == 1)

    for piece in range(1):
        load_a(piece).wait()

    def step_body(g, carry):
        @pl.when((z == 0) & (g < 8))
        def _():
            spread(g * UCH, UCH)
            for t in range(4):
                for j in range(2):
                    x = sf[pl.ds(2 * t + j, UCH, stride=8), :].astype(BF16)
                    uraw[t, pl.ds(pl.multiple_of(g * UCH, UCH), UCH), j * 128:(j + 1) * 128] = x

        for way, hop in ((0, hop_plus), (1, hop_minus)):
            chunk = g - hop
            live = (chunk >= 0) & (chunk < STEPS)

            @pl.when(live & (z != 0))
            def _():
                u_copy(way, chunk).wait_recv()

            @pl.when(live & (hop != NZ - 1))
            def _():
                u_copy(way, chunk).start()

        @pl.when(source & (g < STEPS))
        def _():
            spread(g * 4 * LCH, 4 * LCH)
            for t in range(4):
                x = sf[pl.ds(2 * t, 4 * LCH, stride=8), :].astype(BF16)
                lraw[pl.ds(pl.multiple_of(g * 4 * LCH, 4 * LCH), 4 * LCH), t * 128:(t + 1) * 128] = x

        for k in range(2):
            chunk = g - hops[k]
            live = (chunk >= 0) & (chunk < STEPS)

            @pl.when(live & jnp.logical_not(source))
            def _():
                l_copy(own[k], chunk, sibling, s_send.at[k]).wait_recv()

            for dim in range(4):
                @pl.when(live & sends[k][dim])
                def _():
                    l_copy(own[k], chunk, nears[dim], l_send.at[k, dim]).start()

            @pl.when(live & jnp.logical_not(root_second))
            def _():
                l_copy(own[k], chunk, sibling, s_send.at[k]).start()

        for k in range(2):
            chunk = g - other_hops[k]
            live = (chunk >= 0) & (chunk < STEPS)

            @pl.when(live & jnp.logical_not(source))
            def _():
                l_copy(others[k], chunk, sibling, s_send.at[2 + k]).wait_recv()

            @pl.when(live & source)
            def _():
                l_copy(others[k], chunk, sibling, s_send.at[2 + k]).start()

        @pl.when(g == 1)
        def _():
            for step in range(1, NZ):
                z_copy(step).wait()
            dt[core * 16 + node] = jnp.concatenate([dz[i] for i in range(NZ)], axis=1)
            d_copy(0).start()

        for dim in range(1, 5):
            @pl.when(g == 1 + dim)
            def _():
                d_copy(dim - 1).wait()
                d_copy(dim).start()

        @pl.when((g >= 1) & (g < 6) & source)
        def _():
            load_a(g).wait()

        return carry

    lax.fori_loop(0, STEPS + NZ - 1, step_body, 0)

    d_copy(4).wait()

    @pl.when(jnp.logical_not(source))
    def _():
        for piece in range(1, 6):
            load_a(piece).wait()

    for way, hop in ((0, hop_plus), (1, hop_minus)):
        @pl.when(hop != NZ - 1)
        def _():
            part = uraw.at[pl.ds(2 * way, 2)]
            pltpu.make_async_copy(part, part, u_send.at[way]).wait()

    for k in range(2):
        part = lraw.at[pl.ds(0, STEPS * LCH)]
        for dim in range(4):
            @pl.when(sends[k][dim])
            def _():
                pltpu.make_async_copy(part, part, l_send.at[k, dim]).wait()

        @pl.when(jnp.logical_not(root_second))
        def _():
            pltpu.make_async_copy(part, part, s_send.at[k]).wait()

        @pl.when(source)
        def _():
            pltpu.make_async_copy(part, part, s_send.at[2 + k]).wait()

    for block in range(32):
        dtf[pl.ds(block_column(block) * 16, 16), :] = dt[block].astype(F32)
    packed = dtf[...].T
    row = lax.broadcasted_iota(jnp.int32, (NB, NB), 0)
    column = lax.broadcasted_iota(jnp.int32, (NB, NB), 1)
    uinv[...] = jnp.where(column >= row, packed, 0.0).astype(BF16)
    linv[...] = jnp.where(column < row, packed, jnp.where(column == row, 1.0, 0.0)).astype(BF16)

    for t in range(4):
        ub[t] = jnp.dot(linv[...], uraw[t], preferred_element_type=F32).astype(BF16)

    def update(b, carry):
        first = pl.multiple_of(b * BLK, BLK)
        head = (z == 0) & (b < NB // BLK)

        @pl.when(jnp.logical_not(head))
        def _():
            l = jnp.dot(lraw[pl.ds(first, BLK), :], uinv[...], preferred_element_type=F32).astype(BF16)
            for t in range(4):
                p = jnp.dot(l, ub[t], preferred_element_type=F32)
                for j in range(2):
                    sf[pl.ds(2 * t + j, BLK, stride=8), :] = p[:, j * 128:(j + 1) * 128]

            @pl.when(source)
            def _():
                for t in range(4):
                    sf[pl.ds(2 * t, BLK, stride=8), :] = -l[:, t * 128:(t + 1) * 128].astype(F32)

        @pl.when(head)
        def _():
            for t in range(4):
                for j in range(2):
                    u = ub[t, pl.ds(first, BLK), j * 128:(j + 1) * 128].astype(F32)
                    sf[pl.ds(2 * t + j, BLK, stride=8), :] = -u

            @pl.when(source)
            def _():
                for t in range(4):
                    sf[pl.ds(2 * t, BLK, stride=8), :] = jnp.zeros((BLK, 128), F32)

        keep_even = jnp.where(head == source, 1.0, 0.0)
        keep_odd = jnp.where(head, 0.0, 1.0)
        even = lax.broadcasted_iota(jnp.int32, (8, 128), 0) % 2 == 0
        keep = jnp.where(even, keep_even, keep_odd)
        rows = pl.ds(pl.multiple_of(first * 8, BLK * 8), BLK * 8)
        a = av[rows, :].astype(F32).reshape(BLK, 8, 128) * keep[None]
        out_ref[rows, :] = (a.reshape(BLK * 8, 128) - sf[...]).astype(BF16)
        return carry

    lax.fori_loop(0, ROWS // BLK, update, 0)


def settle(x_ref, out_ref, sem):
    parts = [pl.ds(piece * NB * 8, NB * 8) for piece in range(6)]
    copies = [pltpu.make_async_copy(x_ref.at[part], out_ref.at[part], sem.at[i]) for i, part in enumerate(parts)]
    for copy in copies:
        copy.start()
    for copy in copies:
        copy.wait()


def shards(matrix, diag_inverses):
    flat = matrix.reshape(ROWS, 2, 4, 128).transpose(0, 2, 1, 3).reshape(ROWS * 8, 128)
    dma = pltpu.SemaphoreType.DMA
    out = pl.pallas_call(
        kernel,
        out_shape=jax.ShapeDtypeStruct((ROWS * 8, 128), BF16),
        in_specs=[pl.BlockSpec(memory_space=pltpu.HBM), pl.BlockSpec(memory_space=pltpu.VMEM)],
        out_specs=pl.BlockSpec(memory_space=pltpu.VMEM),
        scratch_shapes=[
            pltpu.VMEM((ROWS * 8, 128), BF16),
            pltpu.VMEM((BLK * 8, 128), F32),
            pltpu.VMEM((ROWS, NB), BF16),
            pltpu.VMEM((4, NB, 256), BF16),
            pltpu.VMEM((4, NB, 256), BF16),
            pltpu.VMEM((NB, NB), BF16),
            pltpu.VMEM((NB, NB), BF16),
            pltpu.VMEM((NZ, 16, 64), BF16),
            pltpu.VMEM((32, 16, NB), BF16),
            pltpu.VMEM((NB, NB), F32),
            dma((6,)),
            dma((2, 4)),
            dma((4, STEPS)),
            dma((4,)),
            dma((2,)),
            dma((2, STEPS)),
            dma((NZ - 1,)),
            dma((NZ - 1,)),
            dma((5,)),
            dma((5,)),
        ],
        compiler_params=pltpu.CompilerParams(
            collective_id=0, has_side_effects=True, vmem_limit_bytes=32 * 2**20),
    )(flat, diag_inverses.T)
    out = pl.pallas_call(
        settle,
        out_shape=jax.ShapeDtypeStruct((ROWS * 8, 128), BF16),
        in_specs=[pl.BlockSpec(memory_space=pl.ANY)],
        out_specs=pl.BlockSpec(memory_space=pl.ANY),
        scratch_shapes=[dma((6,))],
        compiler_params=pltpu.CompilerParams(vmem_limit_bytes=2**20),
    )(out)
    return out.reshape(ROWS, 4, 2, 128).transpose(0, 2, 1, 3).reshape(matrix.shape)


def solution(mesh):
    in_specs = (P(None, "prow", None, "pcol"), P("prow", "pcol"))
    out_specs = P(None, "prow", None, "pcol")
    return jax.shard_map(shards, mesh=mesh, in_specs=in_specs, out_specs=out_specs, check_vma=False)
```

time: 297 us -> 93.5 us (0.31)
  the two profiles are of different devices: /device:TPU:96 before, /device:TPU:32 now
where the time goes in v1:
time: 93.5 us; the launch traced here: 93.4 us
  Pallas kernels  89.9 us (96%)
  local copies, waits for them, and re-layouts  3.47 us (4%)
    pallas_call x1, Pallas kernels, shards(): pl.pallas_call(kernel, out_shape=jax.ShapeDtypeStruct((ROWS * 8, 128), BF...  87.2 us
    unnamed x4, local copies, waits for them, and re-layouts  3.47 us
    pallas_call x1, Pallas kernels, shards(): pl.pallas_call(settle, out_shape=jax.ShapeDtypeStruct((ROWS * 8, 128), BF...  2.72 us

profile of v1, /device:TPU:32, one launch (start us, length us, event | category | flops | bytes accessed | tf_op | source)
XLA Modules:
  0.0 93.4 jit_solution(11875863942596295488)
XLA Ops:
  0.0 0.0 copy-start
  0.0 2.8 %copy-done = bf16[6,512,2,512]{3,2,1,0:T(2,128)(2,1)S(1)} copy-done((bf16[6,512,2,512]{3,2,1,0:T(2,128)(2,1)S(1)}, bf16[6,512,2,512]{3,2,1,0:T(2,128)(2,1)}, u32[]{:S(2)}) %copy-start) | copy-done | bytes 6291480
  2.8 0.0 copy-start.1
  2.8 0.7 copy-done.1
  3.5 87.2 %shard_map.28.x_ref = bf16[24576,128]{1,0:T(8,128)(2,1)S(1)} custom-call(bf16[24576,128]{1,0:T(8,128)(2,1)S(1)} %bitcast.11, bf16[16,64]{1,0:T(8,128)(2,1)S(1)} %bitcast.12), custom_call_target="tpu_custom_call" | custom-call | tf_op jit(solution)/shard_map/pallas_call | solution.py:317
  90.7 2.7 %shard_map.29 = bf16[24576,128]{1,0:T(8,128)(2,1)} custom-call(bf16[24576,128]{1,0:T(8,128)(2,1)S(1)} %shard_map.28.x_ref), custom_call_target="tpu_custom_call" | custom-call | tf_op jit(solution)/shard_map/pallas_call | solution.py:347
Async XLA Ops:
  0.0 2.8 %copy-start = (bf16[6,512,2,512]{3,2,1,0:T(2,128)(2,1)S(1)}, bf16[6,512,2,512]{3,2,1,0:T(2,128)(2,1)}, u32[]{:S(2)}) copy-start(bf16[6,512,2,512]{3,2,1,0:T(2,128)(2,1)} %param.2) | copy-start | bytes 18874372
  2.8 0.7 copy-start.1

commit v2 on v1

v2 whole, which is shorter than its diff:
```python
import jax
import jax.numpy as jnp
from jax import lax
from jax.experimental import pallas as pl
from jax.experimental.pallas import tpu as pltpu
from jax.sharding import PartitionSpec as P

MESH = pl.DeviceIdType.MESH
BF16, F32 = jnp.bfloat16, jnp.float32
NB = 512
ROWS = 6 * NB
NZ = 8
STEPS = 16
LCH = ROWS // (4 * STEPS)
UCH = 64
UPER = NB // UCH
BLK = 256
UHOP, LHOP, CHOP = 6, 6, 3
SLOTS = 4
TOTAL = STEPS + (NZ - 1) * UHOP
DSTEP = 6
INVERT = DSTEP + 4 * LHOP + CHOP
EARLY = max(INVERT, STEPS + NZ // 2 * UHOP)
SOLVE = max(EARLY, 5 * LHOP + 2 * CHOP)
LATE = max(SOLVE + STEPS, UPER + (NZ - 1) * UHOP)
PER = -(-(ROWS // BLK) // (TOTAL - LATE))


def parent(tree, node):
    bit = 1 << tree
    if not node & bit:
        return node | bit
    if node == bit:
        return 0
    for step in range(1, 4):
        other = 1 << ((tree + step) % 4)
        if node & other:
            return node ^ other


def depth(tree, node):
    return 0 if node == 0 else 1 + depth(tree, parent(tree, node))


def table(bits):
    return sum(1 << node for node in range(16) if bits(node))


CHILD = [[table(lambda v: v ^ (1 << j) and parent(i, v ^ (1 << j)) == v) for j in range(4)] for i in range(4)]
DEPTH = [[table(lambda v: (depth(i, v) >> b) & 1) for b in range(3)] for i in range(4)]


def gray_position(code):
    return code ^ (code >> 1)


def block_column(block):
    core, node = divmod(block, 16)
    return gray_position(node % 4) * 8 + gray_position(node // 4) * 2 + core


def kernel(av, d_ref, s_ref, sf, lraw, lsol, uraw, ub, uinv, linv, dz, dt, dtf,
           l_send, l_recv, s_send, u_send, u_recv, z_send, z_recv, d_send, d_recv):
    z = lax.axis_index("prow")
    col = lax.axis_index("pcol")
    core = col % 2
    gx, gy = col // 8, (col // 2) % 4
    gx = gx ^ (gx >> 1)
    gy = gy ^ (gy >> 1)
    node = gx + 4 * gy
    sibling = col + 1 - 2 * core
    source = col == 0
    plain = col != 0

    def near(dim):
        px, py = (gx ^ (1 << dim), gy) if dim < 2 else (gx, gy ^ (1 << (dim - 2)))
        return (px ^ (px >> 1)) * 8 + (py ^ (py >> 1)) * 2 + core

    nears = [near(dim) for dim in range(4)]

    def look(first, second):
        return (jnp.where(core == 0, first, second) >> node) & 1

    barrier = pltpu.get_barrier_semaphore()
    for step in range(1, NZ):
        pl.semaphore_signal(barrier, inc=1, device_id=((z + step) % NZ, col), device_id_type=MESH)
    for other in nears + [sibling]:
        pl.semaphore_signal(barrier, inc=1, device_id=(z, other), device_id_type=MESH)
    pl.semaphore_wait(barrier, NZ + 4)

    def z_copy(step):
        return pltpu.make_async_remote_copy(
            src_ref=d_ref, dst_ref=dz.at[z], send_sem=z_send.at[step - 1], recv_sem=z_recv.at[step - 1],
            device_id=((z + step) % NZ, col), device_id_type=MESH)

    def d_copy(dim):
        if dim < 4:
            base = core * 16 + (node // (1 << dim)) * (1 << dim)
            blocks, target = pl.ds(base, 1 << dim), nears[dim]
        else:
            blocks, target = pl.ds(core * 16, 16), sibling
        return pltpu.make_async_remote_copy(
            src_ref=dt.at[blocks], dst_ref=dt.at[blocks], send_sem=d_send.at[dim], recv_sem=d_recv.at[dim],
            device_id=(z, target), device_id_type=MESH)

    def u_copy(way, chunk):
        target = (z + 1) % NZ if way == 0 else (z + NZ - 1) % NZ
        rows = pl.ds(pl.multiple_of(lax.rem(chunk, UPER) * UCH, UCH), UCH)
        part = uraw.at[2 * way + lax.div(chunk, UPER), rows]
        return pltpu.make_async_remote_copy(
            src_ref=part, dst_ref=part, send_sem=u_send.at[way, lax.rem(chunk, SLOTS)], recv_sem=u_recv.at[way, chunk],
            device_id=(target, col), device_id_type=MESH)

    def l_copy(tree, chunk, target, sem):
        part = lraw.at[pl.ds(pl.multiple_of((chunk * 4 + tree) * LCH, LCH), LCH)]
        return pltpu.make_async_remote_copy(
            src_ref=part, dst_ref=part, send_sem=sem.at[lax.rem(chunk, SLOTS)], recv_sem=l_recv.at[tree, chunk],
            device_id=(z, target), device_id_type=MESH)

    def push(tree, chunk, target, sem):
        @pl.when(chunk >= SLOTS)
        def _():
            l_copy(tree, chunk - SLOTS, target, sem).wait_send()

        l_copy(tree, chunk, target, sem).start()

    def spread(first, rows):
        first = pl.multiple_of(first * 8, 16)
        sf[pl.ds(0, rows * 8), :] = av[pl.ds(first, rows * 8), :].astype(F32)

    hop_plus, hop_minus = z, (NZ - z) % NZ
    own, sends, hops = [], [], []
    others, other_hops = [], []
    for k in range(2):
        own.append(2 * core + k)
        sends.append([look(CHILD[k][dim], CHILD[2 + k][dim]) == 1 for dim in range(4)])
        hops.append(sum(look(DEPTH[k][b], DEPTH[2 + k][b]) << b for b in range(3)) * LHOP + core * CHOP)
        others.append(2 * (1 - core) + k)
        hop = sum(look(DEPTH[2 + k][b], DEPTH[k][b]) << b for b in range(3))
        other_hops.append(jnp.where(source, 0, hop * LHOP + (2 - core) * CHOP))
    to_sibling = jnp.logical_not((node == 0) & (core == 1))
    near_t = jnp.where(z <= NZ // 2, 0, 2)
    far_t = 2 - near_t

    def solve_u(t):
        ub[t] = jnp.dot(linv[...], uraw[t], preferred_element_type=F32).astype(BF16)

    def update(t, first, rows, l):
        p = jnp.dot(l, ub[t], preferred_element_type=F32)
        base = first * 8 + 2 * t

        @pl.when(plain)
        def _():
            s_ref[pl.ds(base, rows, stride=8), :] = p[:, 0:128]

        s_ref[pl.ds(base + 1, rows, stride=8), :] = p[:, 128:256]

    def update_block(t, b):
        first = pl.multiple_of(b * BLK, BLK)
        update(t, first, BLK, lsol[pl.ds(first, BLK), :])

    def step_body(g, carry):
        @pl.when((z == 0) & (g < UPER))
        def _():
            spread(g * UCH, UCH)
            for t in range(4):
                for j in range(2):
                    x = sf[pl.ds(2 * t + j, UCH, stride=8), :].astype(BF16)
                    uraw[t, pl.ds(pl.multiple_of(g * UCH, UCH), UCH), j * 128:(j + 1) * 128] = x

        for way, hop in ((0, hop_plus), (1, hop_minus)):
            chunk = g - hop * UHOP

            @pl.when((chunk >= 0) & (chunk < STEPS))
            def _():
                @pl.when(z != 0)
                def _():
                    u_copy(way, chunk).wait_recv()

                @pl.when(hop != NZ - 1)
                def _():
                    @pl.when(chunk >= SLOTS)
                    def _():
                        u_copy(way, chunk - SLOTS).wait_send()

                    u_copy(way, chunk).start()

        @pl.when(source & (g < STEPS))
        def _():
            spread(g * 4 * LCH, 4 * LCH)
            for t in range(4):
                x = sf[pl.ds(2 * t, 4 * LCH, stride=8), :].astype(BF16)
                lraw[pl.ds(pl.multiple_of(g * 4 * LCH, 4 * LCH), 4 * LCH), t * 128:(t + 1) * 128] = x

        for k in range(2):
            chunk = g - hops[k]

            @pl.when((chunk >= 0) & (chunk < STEPS))
            def _():
                @pl.when(plain)
                def _():
                    l_copy(own[k], chunk, sibling, s_send.at[k]).wait_recv()

                for dim in range(4):
                    @pl.when(sends[k][dim])
                    def _():
                        push(own[k], chunk, nears[dim], l_send.at[k, dim])

                @pl.when(to_sibling)
                def _():
                    push(own[k], chunk, sibling, s_send.at[k])

        for k in range(2):
            chunk = g - other_hops[k]

            @pl.when((chunk >= 0) & (chunk < STEPS))
            def _():
                @pl.when(plain)
                def _():
                    l_copy(others[k], chunk, sibling, s_send.at[2 + k]).wait_recv()

                @pl.when(source)
                def _():
                    push(others[k], chunk, sibling, s_send.at[2 + k])

        @pl.when(g <= INVERT)
        def _():
            @pl.when(g == 0)
            def _():
                for step in range(1, NZ):
                    z_copy(step).start()
                dz[z] = d_ref[...]

            @pl.when(g == DSTEP)
            def _():
                for step in range(1, NZ):
                    z_copy(step).wait()
                dt[core * 16 + node] = jnp.concatenate([dz[i] for i in range(NZ)], axis=1)
                d_copy(0).start()

            for dim in range(1, 5):
                @pl.when(g == DSTEP + LHOP * dim)
                def _():
                    d_copy(dim - 1).wait()
                    d_copy(dim).start()

            @pl.when(g == INVERT)
            def _():
                d_copy(4).wait()
                for block in range(32):
                    dtf[pl.ds(block_column(block) * 16, 16), :] = dt[block].astype(F32)
                packed = dtf[...].T
                row = lax.broadcasted_iota(jnp.int32, (NB, NB), 0)
                column = lax.broadcasted_iota(jnp.int32, (NB, NB), 1)
                uinv[...] = jnp.where(column >= row, packed, 0.0).astype(BF16)
                linv[...] = jnp.where(column < row, packed, jnp.where(column == row, 1.0, 0.0)).astype(BF16)

        @pl.when(g == EARLY)
        def _():
            solve_u(near_t)
            solve_u(near_t + 1)

        @pl.when((g >= SOLVE) & (g < SOLVE + STEPS))
        def _():
            first = pl.multiple_of((g - SOLVE) * 4 * LCH, 4 * LCH)
            rows = pl.ds(first, 4 * LCH)
            l = jnp.dot(lraw[rows, :], uinv[...], preferred_element_type=F32).astype(BF16)
            lsol[rows, :] = l
            update(near_t, first, 4 * LCH, l)
            update(near_t + 1, first, 4 * LCH, l)

            @pl.when(source)
            def _():
                for t in range(4):
                    s_ref[pl.ds(first * 8 + 2 * t, 4 * LCH, stride=8), :] = -l[:, t * 128:(t + 1) * 128].astype(F32)

        @pl.when(g >= LATE)
        def _():
            @pl.when(g == LATE)
            def _():
                solve_u(far_t)

            for i in range(PER):
                b = (g - LATE) * PER + i

                @pl.when(b < ROWS // BLK)
                def _():
                    update_block(far_t, b)

        return carry

    lax.fori_loop(0, TOTAL, step_body, 0)

    solve_u(far_t + 1)

    def last_body(b, carry):
        update_block(far_t + 1, b)
        return carry

    lax.fori_loop(0, ROWS // BLK, last_body, 0)

    @pl.when(z == 0)
    def _():
        for t in range(4):
            s_ref[pl.ds(2 * t, NB, stride=8), :] = jnp.where(source, 0.0, -ub[t, :, 0:128].astype(F32))
            s_ref[pl.ds(2 * t + 1, NB, stride=8), :] = -ub[t, :, 128:256].astype(F32)

    def drain(last, carry):
        for way, hop in ((0, hop_plus), (1, hop_minus)):
            @pl.when(hop != NZ - 1)
            def _():
                u_copy(way, last).wait_send()

        for k in range(2):
            for dim in range(4):
                @pl.when(sends[k][dim])
                def _():
                    l_copy(own[k], last, nears[dim], l_send.at[k, dim]).wait_send()

            @pl.when(to_sibling)
            def _():
                l_copy(own[k], last, sibling, s_send.at[k]).wait_send()

            @pl.when(source)
            def _():
                l_copy(others[k], last, sibling, s_send.at[2 + k]).wait_send()

        return carry

    lax.fori_loop(STEPS - SLOTS, STEPS, drain, 0)


def settle(s_ref, a_ref, out_ref, buf, sem):
    z = lax.axis_index("prow")
    source = lax.axis_index("pcol") == 0
    even = lax.broadcasted_iota(jnp.int32, (8, 128), 0) % 2 == 0
    size = BLK * 8

    def copy(b):
        rows = pl.ds(pl.multiple_of(b * size, size), size)
        return pltpu.make_async_copy(buf.at[rows], out_ref.at[rows], sem.at[b])

    def body(b, carry):
        head = (z == 0) & (b < NB // BLK)
        keep_even = jnp.where(head == source, 1.0, 0.0)
        keep_odd = jnp.where(head, 0.0, 1.0)
        keep = jnp.where(even, keep_even, keep_odd)
        rows = pl.ds(pl.multiple_of(b * size, size), size)
        a = a_ref[rows, :].astype(F32).reshape(BLK, 8, 128) * keep[None]
        buf[rows, :] = (a.reshape(size, 128) - s_ref[rows, :]).astype(BF16)
        copy(b).start()
        return carry

    def finish(b, carry):
        copy(b).wait()
        return carry

    lax.fori_loop(0, ROWS // BLK, body, 0)
    lax.fori_loop(0, ROWS // BLK, finish, 0)


def shards(matrix, diag_inverses):
    flat = matrix.reshape(ROWS, 2, 4, 128).transpose(0, 2, 1, 3).reshape(ROWS * 8, 128)
    dma = pltpu.SemaphoreType.DMA
    vmem = pl.BlockSpec(memory_space=pltpu.VMEM)
    product = pl.pallas_call(
        kernel,
        out_shape=jax.ShapeDtypeStruct((ROWS * 8, 128), F32),
        in_specs=[vmem, vmem],
        out_specs=vmem,
        scratch_shapes=[
            pltpu.VMEM((4 * LCH * 8, 128), F32),
            pltpu.VMEM((ROWS, NB), BF16),
            pltpu.VMEM((ROWS, NB), BF16),
            pltpu.VMEM((4, NB, 256), BF16),
            pltpu.VMEM((4, NB, 256), BF16),
            pltpu.VMEM((NB, NB), BF16),
            pltpu.VMEM((NB, NB), BF16),
            pltpu.VMEM((NZ, 16, 64), BF16),
            pltpu.VMEM((32, 16, NB), BF16),
            pltpu.VMEM((NB, NB), F32),
            dma((2, 4, SLOTS)),
            dma((4, STEPS)),
            dma((4, SLOTS)),
            dma((2, SLOTS)),
            dma((2, STEPS)),
            dma((NZ - 1,)),
            dma((NZ - 1,)),
            dma((5,)),
            dma((5,)),
        ],
        compiler_params=pltpu.CompilerParams(
            collective_id=0, has_side_effects=True, vmem_limit_bytes=20 * 2**20),
    )(flat, diag_inverses.T)
    out = pl.pallas_call(
        settle,
        out_shape=jax.ShapeDtypeStruct((ROWS * 8, 128), BF16),
        in_specs=[vmem, vmem],
        out_specs=pl.BlockSpec(memory_space=pl.ANY),
        scratch_shapes=[pltpu.VMEM((ROWS * 8, 128), BF16), dma((ROWS // BLK,))],
        compiler_params=pltpu.CompilerParams(vmem_limit_bytes=12 * 2**20),
    )(product, flat)
    return out.reshape(ROWS, 4, 2, 128).transpose(0, 2, 1, 3).reshape(matrix.shape)


def solution(mesh):
    in_specs = (P(None, "prow", None, "pcol"), P("prow", "pcol"))
    out_specs = P(None, "prow", None, "pcol")
    return jax.shard_map(shards, mesh=mesh, in_specs=in_specs, out_specs=out_specs, check_vma=False)
```

time: 93.5 us -> 64.3 us (0.69)
  the two profiles are of different devices: /device:TPU:32 before, /device:TPU:96 now
where the time goes in v2:
time: 64.3 us; the launch traced here: 63.7 us
  Pallas kernels  60.2 us (94%)
  local copies, waits for them, and re-layouts  3.47 us (5%)
    pallas_call x1, Pallas kernels, shards(): pl.pallas_call(kernel, out_shape=jax.ShapeDtypeStruct((ROWS * 8, 128), F3...  57.3 us
    unnamed x4, local copies, waits for them, and re-layouts  3.47 us
    pallas_call x1, Pallas kernels, shards(): pl.pallas_call(settle, out_shape=jax.ShapeDtypeStruct((ROWS * 8, 128), BF...  2.93 us

profile of v2, /device:TPU:96, one launch (start us, length us, event | category | flops | bytes accessed | tf_op | source)
XLA Modules:
  0.0 63.7 jit_solution(4058075812809855318)
XLA Ops:
  0.0 0.0 copy-start
  0.0 2.8 %copy-done = bf16[6,512,2,512]{3,2,1,0:T(2,128)(2,1)S(1)} copy-done((bf16[6,512,2,512]{3,2,1,0:T(2,128)(2,1)S(1)}, bf16[6,512,2,512]{3,2,1,0:T(2,128)(2,1)}, u32[]{:S(2)}) %copy-start) | copy-done | bytes 6291480
  2.8 0.0 copy-start.1
  2.8 0.7 %copy-done.1 = bf16[64,16]{0,1:T(8,128)(2,1)S(1)} copy-done((bf16[64,16]{0,1:T(8,128)(2,1)S(1)}, bf16[64,16]{0,1:T(8,128)(2,1)}, u32[]{:S(2)}) %copy-start.1) | copy-done | bytes 2072
  3.5 57.3 %shard_map.28.s_ref = f32[24576,128]{1,0:T(8,128)S(1)} custom-call(bf16[24576,128]{1,0:T(8,128)(2,1)S(1)} %bitcast.11, bf16[16,64]{1,0:T(8,128)(2,1)S(1)} %bitcast.13), custom_call_target="tpu_custom_call" | custom-call | tf_op jit(solution)/shard_map/pallas_call | solution.py:366
  60.8 2.9 %shard_map.29 = bf16[24576,128]{1,0:T(8,128)(2,1)} custom-call(f32[24576,128]{1,0:T(8,128)S(1)} %shard_map.28.s_ref, bf16[24576,128]{1,0:T(8,128)(2,1)S(1)} %bitcast.12), custom_call_target="tpu_custom_call" | custom-call | tf_op jit(solution)/shard_map/pallas_call | solution.py:395
Async XLA Ops:
  0.0 2.8 %copy-start = (bf16[6,512,2,512]{3,2,1,0:T(2,128)(2,1)S(1)}, bf16[6,512,2,512]{3,2,1,0:T(2,128)(2,1)}, u32[]{:S(2)}) copy-start(bf16[6,512,2,512]{3,2,1,0:T(2,128)(2,1)} %param.2) | copy-start | bytes 18874372
  2.8 0.7 %copy-start.1 = (bf16[64,16]{0,1:T(8,128)(2,1)S(1)}, bf16[64,16]{0,1:T(8,128)(2,1)}, u32[]{:S(2)}) copy-start(bf16[64,16]{0,1:T(8,128)(2,1)} %param.3) | copy-start | bytes 6148

commit v3 on v2

--- a/solution.py
+++ b/solution.py
@@ -1,3 +1,5 @@
+import functools
+
 import jax
 import jax.numpy as jnp
 from jax import lax
@@ -11,19 +13,20 @@
 ROWS = 6 * NB
 NZ = 8
 STEPS = 16
-LCH = ROWS // (4 * STEPS)
-UCH = 64
+LSTEPS = 12
+LCH = ROWS // (4 * LSTEPS)
+UCH = 2 * NB // STEPS
 UPER = NB // UCH
-BLK = 256
+BLK = 512
 UHOP, LHOP, CHOP = 6, 6, 3
+JUMP = 7
 SLOTS = 4
-TOTAL = STEPS + (NZ - 1) * UHOP
-DSTEP = 6
-INVERT = DSTEP + 4 * LHOP + CHOP
-EARLY = max(INVERT, STEPS + NZ // 2 * UHOP)
-SOLVE = max(EARLY, 5 * LHOP + 2 * CHOP)
-LATE = max(SOLVE + STEPS, UPER + (NZ - 1) * UHOP)
-PER = -(-(ROWS // BLK) // (TOTAL - LATE))
+TOTAL = max(UPER + (NZ - 1) * UHOP, STEPS + 3 * JUMP + UHOP)
+DSTEP, DHOP = 4, 4
+INVERT = DSTEP + 4 * DHOP + 2
+PAIR = 8 * LCH
+OUT = 256
+PER = 3
 
 
 def parent(tree, node):
@@ -103,12 +106,12 @@
             src_ref=dt.at[blocks], dst_ref=dt.at[blocks], send_sem=d_send.at[dim], recv_sem=d_recv.at[dim],
             device_id=(z, target), device_id_type=MESH)
 
-    def u_copy(way, chunk):
-        target = (z + 1) % NZ if way == 0 else (z + NZ - 1) % NZ
+    def u_copy(way, chunk, ahead=1, kind=0):
+        target = (z + ahead) % NZ if way == 0 else (z + NZ - ahead) % NZ
         rows = pl.ds(pl.multiple_of(lax.rem(chunk, UPER) * UCH, UCH), UCH)
         part = uraw.at[2 * way + lax.div(chunk, UPER), rows]
         return pltpu.make_async_remote_copy(
-            src_ref=part, dst_ref=part, send_sem=u_send.at[way, lax.rem(chunk, SLOTS)], recv_sem=u_recv.at[way, chunk],
+            src_ref=part, dst_ref=part, send_sem=u_send.at[kind, way, lax.rem(chunk, SLOTS)], recv_sem=u_recv.at[way, chunk],
             device_id=(target, col), device_id_type=MESH)
 
     def l_copy(tree, chunk, target, sem):
@@ -129,6 +132,12 @@
         sf[pl.ds(0, rows * 8), :] = av[pl.ds(first, rows * 8), :].astype(F32)
 
     hop_plus, hop_minus = z, (NZ - z) % NZ
+    ways = ((0, hop_plus), (1, hop_minus))
+
+    def skip_delay(hop):
+        jumps = jnp.where(hop == NZ - 1, 3, lax.div(hop + 1, 2))
+        return jumps * JUMP + lax.rem(hop, 2) * UHOP
+
     own, sends, hops = [], [], []
     others, other_hops = [], []
     for k in range(2):
@@ -139,6 +148,10 @@
         hop = sum(look(DEPTH[2 + k][b], DEPTH[k][b]) << b for b in range(3))
         other_hops.append(jnp.where(source, 0, hop * LHOP + (2 - core) * CHOP))
     to_sibling = jnp.logical_not((node == 0) & (core == 1))
+    near_hop = jnp.minimum(hop_plus, hop_minus)
+    early = jnp.maximum(INVERT, jnp.maximum(UPER + near_hop * UHOP, STEPS + skip_delay(near_hop)))
+    solve = jnp.maximum(early, functools.reduce(jnp.maximum, hops + other_hops))
+    late = jnp.maximum(solve + LSTEPS, STEPS + skip_delay(jnp.maximum(hop_plus, hop_minus)))
     near_t = jnp.where(z <= NZ // 2, 0, 2)
     far_t = 2 - near_t
 
@@ -168,10 +181,10 @@
                     x = sf[pl.ds(2 * t + j, UCH, stride=8), :].astype(BF16)
                     uraw[t, pl.ds(pl.multiple_of(g * UCH, UCH), UCH), j * 128:(j + 1) * 128] = x
 
-        for way, hop in ((0, hop_plus), (1, hop_minus)):
+        for way, hop in ways:
             chunk = g - hop * UHOP
 
-            @pl.when((chunk >= 0) & (chunk < STEPS))
+            @pl.when((chunk >= 0) & (chunk < UPER))
             def _():
                 @pl.when(z != 0)
                 def _():
@@ -185,7 +198,33 @@
 
                     u_copy(way, chunk).start()
 
-        @pl.when(source & (g < STEPS))
+            skip = g - skip_delay(hop)
+
+            @pl.when((skip >= UPER) & (skip < STEPS))
+            def _():
+                @pl.when(z != 0)
+                def _():
+                    u_copy(way, skip).wait_recv()
+
+                @pl.when(lax.rem(hop, 2) == 0)
+                def _():
+                    ahead = jnp.where(hop == NZ - 2, 1, 2)
+
+                    @pl.when(skip >= UPER + SLOTS)
+                    def _():
+                        u_copy(way, skip - SLOTS, ahead, 1).wait_send()
+
+                    u_copy(way, skip, ahead, 1).start()
+
+                    @pl.when(hop != 0)
+                    def _():
+                        @pl.when(skip >= UPER + SLOTS)
+                        def _():
+                            u_copy(way, skip - SLOTS, NZ - 1, 2).wait_send()
+
+                        u_copy(way, skip, NZ - 1, 2).start()
+
+        @pl.when(source & (g < LSTEPS))
         def _():
             spread(g * 4 * LCH, 4 * LCH)
             for t in range(4):
@@ -195,7 +234,7 @@
         for k in range(2):
             chunk = g - hops[k]
 
-            @pl.when((chunk >= 0) & (chunk < STEPS))
+            @pl.when((chunk >= 0) & (chunk < LSTEPS))
             def _():
                 @pl.when(plain)
                 def _():
@@ -213,7 +252,7 @@
         for k in range(2):
             chunk = g - other_hops[k]
 
-            @pl.when((chunk >= 0) & (chunk < STEPS))
+            @pl.when((chunk >= 0) & (chunk < LSTEPS))
             def _():
                 @pl.when(plain)
                 def _():
@@ -239,7 +278,7 @@
                 d_copy(0).start()
 
             for dim in range(1, 5):
-                @pl.when(g == DSTEP + LHOP * dim)
+                @pl.when(g == (DSTEP + DHOP * dim))
                 def _():
                     d_copy(dim - 1).wait()
                     d_copy(dim).start()
@@ -255,46 +294,44 @@
                 uinv[...] = jnp.where(column >= row, packed, 0.0).astype(BF16)
                 linv[...] = jnp.where(column < row, packed, jnp.where(column == row, 1.0, 0.0)).astype(BF16)
 
-        @pl.when(g == EARLY)
+        @pl.when(g == early)
         def _():
             solve_u(near_t)
             solve_u(near_t + 1)
 
-        @pl.when((g >= SOLVE) & (g < SOLVE + STEPS))
-        def _():
-            first = pl.multiple_of((g - SOLVE) * 4 * LCH, 4 * LCH)
-            rows = pl.ds(first, 4 * LCH)
+        part = g - solve
+
+        @pl.when((part >= 0) & (part < LSTEPS) & (lax.rem(part, 2) == 1))
+        def _():
+            first = pl.multiple_of(lax.div(part, 2) * PAIR, PAIR)
+            rows = pl.ds(first, PAIR)
             l = jnp.dot(lraw[rows, :], uinv[...], preferred_element_type=F32).astype(BF16)
             lsol[rows, :] = l
-            update(near_t, first, 4 * LCH, l)
-            update(near_t + 1, first, 4 * LCH, l)
+            update(near_t, first, PAIR, l)
+            update(near_t + 1, first, PAIR, l)
 
             @pl.when(source)
             def _():
                 for t in range(4):
-                    s_ref[pl.ds(first * 8 + 2 * t, 4 * LCH, stride=8), :] = -l[:, t * 128:(t + 1) * 128].astype(F32)
-
-        @pl.when(g >= LATE)
-        def _():
-            @pl.when(g == LATE)
-            def _():
-                solve_u(far_t)
+                    s_ref[pl.ds(first * 8 + 2 * t, PAIR, stride=8), :] = -l[:, t * 128:(t + 1) * 128].astype(F32)
+
+        @pl.when((g >= late) & (g < late + ROWS // BLK // PER))
+        def _():
+            @pl.when(g == late)
+            def _():
+                solve_u(far_t + 1)
 
             for i in range(PER):
-                b = (g - LATE) * PER + i
-
-                @pl.when(b < ROWS // BLK)
-                def _():
-                    update_block(far_t, b)
+                update_block(far_t + 1, (g - late) * PER + i)
 
         return carry
 
     lax.fori_loop(0, TOTAL, step_body, 0)
 
-    solve_u(far_t + 1)
+    solve_u(far_t)
 
     def last_body(b, carry):
-        update_block(far_t + 1, b)
+        update_block(far_t, b)
         return carry
 
     lax.fori_loop(0, ROWS // BLK, last_body, 0)
@@ -305,11 +342,19 @@
             s_ref[pl.ds(2 * t, NB, stride=8), :] = jnp.where(source, 0.0, -ub[t, :, 0:128].astype(F32))
             s_ref[pl.ds(2 * t + 1, NB, stride=8), :] = -ub[t, :, 128:256].astype(F32)
 
-    def drain(last, carry):
-        for way, hop in ((0, hop_plus), (1, hop_minus)):
+    for last in range(SLOTS):
+        for way, hop in ways:
             @pl.when(hop != NZ - 1)
             def _():
                 u_copy(way, last).wait_send()
+
+            @pl.when(lax.rem(hop, 2) == 0)
+            def _():
+                u_copy(way, last, 2, 1).wait_send()
+
+                @pl.when(hop != 0)
+                def _():
+                    u_copy(way, last, NZ - 1, 2).wait_send()
 
         for k in range(2):
             for dim in range(4):
@@ -324,29 +369,25 @@
             @pl.when(source)
             def _():
                 l_copy(others[k], last, sibling, s_send.at[2 + k]).wait_send()
-
-        return carry
-
-    lax.fori_loop(STEPS - SLOTS, STEPS, drain, 0)
 
 
 def settle(s_ref, a_ref, out_ref, buf, sem):
     z = lax.axis_index("prow")
     source = lax.axis_index("pcol") == 0
     even = lax.broadcasted_iota(jnp.int32, (8, 128), 0) % 2 == 0
-    size = BLK * 8
+    size = OUT * 8
 
     def copy(b):
         rows = pl.ds(pl.multiple_of(b * size, size), size)
         return pltpu.make_async_copy(buf.at[rows], out_ref.at[rows], sem.at[b])
 
     def body(b, carry):
-        head = (z == 0) & (b < NB // BLK)
+        head = (z == 0) & (b < NB // OUT)
         keep_even = jnp.where(head == source, 1.0, 0.0)
         keep_odd = jnp.where(head, 0.0, 1.0)
         keep = jnp.where(even, keep_even, keep_odd)
         rows = pl.ds(pl.multiple_of(b * size, size), size)
-        a = a_ref[rows, :].astype(F32).reshape(BLK, 8, 128) * keep[None]
+        a = a_ref[rows, :].astype(F32).reshape(OUT, 8, 128) * keep[None]
         buf[rows, :] = (a.reshape(size, 128) - s_ref[rows, :]).astype(BF16)
         copy(b).start()
         return carry
@@ -355,8 +396,8 @@
         copy(b).wait()
         return carry
 
-    lax.fori_loop(0, ROWS // BLK, body, 0)
-    lax.fori_loop(0, ROWS // BLK, finish, 0)
+    lax.fori_loop(0, ROWS // OUT, body, 0)
+    lax.fori_loop(0, ROWS // OUT, finish, 0)
 
 
 def shards(matrix, diag_inverses):
@@ -380,9 +421,9 @@
             pltpu.VMEM((32, 16, NB), BF16),
             pltpu.VMEM((NB, NB), F32),
             dma((2, 4, SLOTS)),
-            dma((4, STEPS)),
+            dma((4, LSTEPS)),
             dma((4, SLOTS)),
-            dma((2, SLOTS)),
+            dma((3, 2, SLOTS)),
             dma((2, STEPS)),
             dma((NZ - 1,)),
             dma((NZ - 1,)),
@@ -397,7 +438,7 @@
         out_shape=jax.ShapeDtypeStruct((ROWS * 8, 128), BF16),
         in_specs=[vmem, vmem],
         out_specs=pl.BlockSpec(memory_space=pl.ANY),
-        scratch_shapes=[pltpu.VMEM((ROWS * 8, 128), BF16), dma((ROWS // BLK,))],
+        scratch_shapes=[pltpu.VMEM((ROWS * 8, 128), BF16), dma((ROWS // OUT,))],
         compiler_params=pltpu.CompilerParams(vmem_limit_bytes=12 * 2**20),
     )(product, flat)
     return out.reshape(ROWS, 4, 2, 128).transpose(0, 2, 1, 3).reshape(matrix.shape)

time: 64.3 us -> 73.2 us (1.14)
  Pallas kernels: 60.2 us -> 69.6 us
    pallas_call x1, Pallas kernels: 57.3 us -> 66.7 us  [shards(): pl.pallas_call(kernel, out_shape=jax.ShapeDtypeStruct((ROWS * 8, 128), F3...]
where the time goes in v3:
time: 73.2 us; the launch traced here: 73.1 us
  Pallas kernels  69.6 us (95%)
  local copies, waits for them, and re-layouts  3.47 us (5%)
    pallas_call x1, Pallas kernels, shards(): pl.pallas_call(kernel, out_shape=jax.ShapeDtypeStruct((ROWS * 8, 128), F3...  66.7 us
    unnamed x4, local copies, waits for them, and re-layouts  3.47 us
    pallas_call x1, Pallas kernels, shards(): pl.pallas_call(settle, out_shape=jax.ShapeDtypeStruct((ROWS * 8, 128), BF...  2.93 us

profile of v3, /device:TPU:96, one launch (start us, length us, event | category | flops | bytes accessed | tf_op | source)
XLA Modules:
  0.0 73.1 jit_solution(11683864671441481858)
XLA Ops:
  0.0 0.0 copy-start
  0.0 2.8 %copy-done = bf16[6,512,2,512]{3,2,1,0:T(2,128)(2,1)S(1)} copy-done((bf16[6,512,2,512]{3,2,1,0:T(2,128)(2,1)S(1)}, bf16[6,512,2,512]{3,2,1,0:T(2,128)(2,1)}, u32[]{:S(2)}) %copy-start) | copy-done | bytes 6291480
  2.8 0.0 copy-start.1
  2.8 0.7 copy-done.1
  3.5 66.7 %shard_map.28.s_ref = f32[24576,128]{1,0:T(8,128)S(1)} custom-call(bf16[24576,128]{1,0:T(8,128)(2,1)S(1)} %bitcast.11, bf16[16,64]{1,0:T(8,128)(2,1)S(1)} %bitcast.13), custom_call_target="tpu_custom_call" | custom-call | tf_op jit(solution)/shard_map/pallas_call | solution.py:407
  70.2 2.9 %shard_map.29 = bf16[24576,128]{1,0:T(8,128)(2,1)} custom-call(f32[24576,128]{1,0:T(8,128)S(1)} %shard_map.28.s_ref, bf16[24576,128]{1,0:T(8,128)(2,1)S(1)} %bitcast.12), custom_call_target="tpu_custom_call" | custom-call | tf_op jit(solution)/shard_map/pallas_call | solution.py:436
Async XLA Ops:
  0.0 2.8 %copy-start = (bf16[6,512,2,512]{3,2,1,0:T(2,128)(2,1)S(1)}, bf16[6,512,2,512]{3,2,1,0:T(2,128)(2,1)}, u32[]{:S(2)}) copy-start(bf16[6,512,2,512]{3,2,1,0:T(2,128)(2,1)} %param.2) | copy-start | bytes 18874372
  2.8 0.7 copy-start.1

commit v4 on v3

v4 whole, which is shorter than its diff:
```python
import functools

import jax
import jax.numpy as jnp
from jax import lax
from jax.experimental import pallas as pl
from jax.experimental.pallas import tpu as pltpu
from jax.sharding import PartitionSpec as P

MESH = pl.DeviceIdType.MESH
BF16, F32 = jnp.bfloat16, jnp.float32
NB = 512
ROWS = 6 * NB
NZ = 8
STEPS = 16
LSTEPS = 12
LCH = ROWS // (4 * LSTEPS)
UCH = 2 * NB // STEPS
UPER = NB // UCH
BLK = 512
UHOP, LHOP, CHOP = 6, 6, 3
SLOTS = 4
TOTAL = STEPS + (NZ - 1) * UHOP
DSTEP, DHOP = 6, 6
INVERT = DSTEP + 2 * DHOP + 3
OUT = 256
ITEMS = 3 * (ROWS // BLK)
PER = 3


def parent(tree, node):
    bit = 1 << tree
    if not node & bit:
        return node | bit
    if node == bit:
        return 0
    for step in range(1, 4):
        other = 1 << ((tree + step) % 4)
        if node & other:
            return node ^ other


def depth(tree, node):
    return 0 if node == 0 else 1 + depth(tree, parent(tree, node))


def table(bits):
    return sum(1 << node for node in range(16) if bits(node))


CHILD = [[table(lambda v: v ^ (1 << j) and parent(i, v ^ (1 << j)) == v) for j in range(4)] for i in range(4)]
DEPTH = [[table(lambda v: (depth(i, v) >> b) & 1) for b in range(3)] for i in range(4)]


def gray_position(code):
    return code ^ (code >> 1)


def block_column(block):
    core, node = divmod(block, 16)
    return gray_position(node % 4) * 8 + gray_position(node // 4) * 2 + core


def kernel(a_ref, d_ref, s_low, s_high, av, sf, lraw, lsol, uraw, ub, uinv, linv, dz, dt, dtf,
           a_sem, l_send, l_recv, s_send, u_send, u_recv, z_send, z_recv, d_send, d_recv):
    z = lax.axis_index("prow")
    col = lax.axis_index("pcol")
    core = col % 2
    gx, gy = col // 8, (col // 2) % 4
    gx = gx ^ (gx >> 1)
    gy = gy ^ (gy >> 1)
    node = gx + 4 * gy
    sibling = col + 1 - 2 * core
    source = col == 0
    plain = col != 0

    def place(px, py):
        return (px ^ (px >> 1)) * 8 + (py ^ (py >> 1)) * 2 + core

    across = {k: place(gx ^ k, gy) for k in range(1, 4)}
    across.update({4 + k: place(gx, gy ^ k) for k in range(1, 4)})
    nears = [across[1], across[2], across[5], across[6]]

    def look(first, second):
        return (jnp.where(core == 0, first, second) >> node) & 1

    def load_a(piece):
        rows = pl.ds(pl.multiple_of(piece * (NB * 8), NB * 8), NB * 8)
        return pltpu.make_async_copy(a_ref.at[rows], av.at[rows], a_sem.at[piece])

    for piece in range(6):
        load_a(piece).start()

    barrier = pltpu.get_barrier_semaphore()
    for step in range(1, NZ):
        pl.semaphore_signal(barrier, inc=1, device_id=((z + step) % NZ, col), device_id_type=MESH)
    for other in list(across.values()) + [sibling]:
        pl.semaphore_signal(barrier, inc=1, device_id=(z, other), device_id_type=MESH)
    pl.semaphore_wait(barrier, NZ + 6)

    def z_copy(step):
        return pltpu.make_async_remote_copy(
            src_ref=d_ref, dst_ref=dz.at[z], send_sem=z_send.at[step - 1], recv_sem=z_recv.at[step - 1],
            device_id=((z + step) % NZ, col), device_id_type=MESH)

    def d_copy(stage, k=1):
        if stage == 0:
            blocks, target = pl.ds(core * 16 + node, 1), across[k]
        elif stage == 1:
            blocks, target = pl.ds(core * 16 + gy * 4, 4), across[4 + k]
        else:
            blocks, target = pl.ds(core * 16, 16), sibling
        return pltpu.make_async_remote_copy(
            src_ref=dt.at[blocks], dst_ref=dt.at[blocks], send_sem=d_send.at[stage, k], recv_sem=d_recv.at[stage, k],
            device_id=(z, target), device_id_type=MESH)

    def u_copy(way, chunk):
        target = (z + 1) % NZ if way == 0 else (z + NZ - 1) % NZ
        rows = pl.ds(pl.multiple_of(lax.rem(chunk, UPER) * UCH, UCH), UCH)
        part = uraw.at[2 * way + lax.div(chunk, UPER), rows]
        return pltpu.make_async_remote_copy(
            src_ref=part, dst_ref=part, send_sem=u_send.at[way, lax.rem(chunk, SLOTS)], recv_sem=u_recv.at[way, chunk],
            device_id=(target, col), device_id_type=MESH)

    def l_copy(tree, chunk, target, sem):
        part = lraw.at[pl.ds(pl.multiple_of((chunk * 4 + tree) * LCH, LCH), LCH)]
        return pltpu.make_async_remote_copy(
            src_ref=part, dst_ref=part, send_sem=sem.at[lax.rem(chunk, SLOTS)], recv_sem=l_recv.at[tree, chunk],
            device_id=(z, target), device_id_type=MESH)

    def push(tree, chunk, target, sem):
        @pl.when(chunk >= SLOTS)
        def _():
            l_copy(tree, chunk - SLOTS, target, sem).wait_send()

        l_copy(tree, chunk, target, sem).start()

    def spread(first, rows):
        first = pl.multiple_of(first * 8, 16)
        sf[pl.ds(0, rows * 8), :] = av[pl.ds(first, rows * 8), :].astype(F32)

    hop_plus, hop_minus = z, (NZ - z) % NZ
    ways = ((0, hop_plus), (1, hop_minus))

    own, sends, hops = [], [], []
    others, other_hops = [], []
    for k in range(2):
        own.append(2 * core + k)
        sends.append([look(CHILD[k][dim], CHILD[2 + k][dim]) == 1 for dim in range(4)])
        hops.append(sum(look(DEPTH[k][b], DEPTH[2 + k][b]) << b for b in range(3)) * LHOP + core * CHOP)
        others.append(2 * (1 - core) + k)
        hop = sum(look(DEPTH[2 + k][b], DEPTH[k][b]) << b for b in range(3))
        other_hops.append(jnp.where(source, 0, hop * LHOP + (2 - core) * CHOP))
    to_sibling = jnp.logical_not((node == 0) & (core == 1))
    near_hop = jnp.minimum(hop_plus, hop_minus)
    middle = z == NZ // 2
    early = jnp.maximum(INVERT, jnp.where(middle, UPER, STEPS) + near_hop * UHOP)
    solve = jnp.maximum(early, functools.reduce(jnp.maximum, hops + other_hops) + BLK // (4 * LCH) - 1)
    late = jnp.maximum(solve + ITEMS, UPER + jnp.maximum(hop_plus, hop_minus) * UHOP)
    near_t = jnp.where(z <= NZ // 2, 0, 2)
    far_t = 2 - near_t
    order = [near_t, jnp.where(middle, 2, near_t + 1), jnp.where(middle, 1, far_t), far_t + 1]

    def solve_u(t):
        ub[t] = jnp.dot(linv[...], uraw[t], preferred_element_type=F32).astype(BF16)

    def store(first, offset, value):
        for half, ref in enumerate((s_low, s_high)):
            @pl.when((first >= ROWS // 2) == (half == 1))
            def _():
                ref[pl.ds((first - half * (ROWS // 2)) * 8 + offset, BLK, stride=8), :] = value

    def update(t, first, l):
        p = jnp.dot(l, ub[t], preferred_element_type=F32)

        @pl.when(plain)
        def _():
            store(first, 2 * t, p[:, 0:128])

        store(first, 2 * t + 1, p[:, 128:256])

    def update_block(t, b):
        first = pl.multiple_of(b * BLK, BLK)
        update(t, first, lsol[pl.ds(first, BLK), :])

    load_a(0).wait()

    def step_body(g, carry):
        @pl.when((z == 0) & (g < UPER))
        def _():
            spread(g * UCH, UCH)
            for t in range(4):
                for j in range(2):
                    x = sf[pl.ds(2 * t + j, UCH, stride=8), :].astype(BF16)
                    uraw[t, pl.ds(pl.multiple_of(g * UCH, UCH), UCH), j * 128:(j + 1) * 128] = x

        for way, hop in ways:
            chunk = g - hop * UHOP

            @pl.when((chunk >= 0) & (chunk < STEPS))
            def _():
                @pl.when(z != 0)
                def _():
                    u_copy(way, chunk).wait_recv()

                @pl.when(hop != NZ - 1)
                def _():
                    @pl.when(chunk >= SLOTS)
                    def _():
                        u_copy(way, chunk - SLOTS).wait_send()

                    u_copy(way, chunk).start()

        @pl.when(source & (g < LSTEPS))
        def _():
            spread(g * 4 * LCH, 4 * LCH)
            for t in range(4):
                x = sf[pl.ds(2 * t, 4 * LCH, stride=8), :].astype(BF16)
                lraw[pl.ds(pl.multiple_of(g * 4 * LCH, 4 * LCH), 4 * LCH), t * 128:(t + 1) * 128] = x

        for k in range(2):
            chunk = g - hops[k]

            @pl.when((chunk >= 0) & (chunk < LSTEPS))
            def _():
                @pl.when(plain)
                def _():
                    l_copy(own[k], chunk, sibling, s_send.at[k]).wait_recv()

                for dim in range(4):
                    @pl.when(sends[k][dim])
                    def _():
                        push(own[k], chunk, nears[dim], l_send.at[k, dim])

                @pl.when(to_sibling)
                def _():
                    push(own[k], chunk, sibling, s_send.at[k])

        for k in range(2):
            chunk = g - other_hops[k]

            @pl.when((chunk >= 0) & (chunk < LSTEPS))
            def _():
                @pl.when(plain)
                def _():
                    l_copy(others[k], chunk, sibling, s_send.at[2 + k]).wait_recv()

                @pl.when(source)
                def _():
                    push(others[k], chunk, sibling, s_send.at[2 + k])

        @pl.when(g <= INVERT)
        def _():
            @pl.when((g >= 1) & (g < 6))
            def _():
                load_a(g).wait()

            @pl.when(g == 0)
            def _():
                for step in range(1, NZ):
                    z_copy(step).start()
                dz[z] = d_ref[...]

            @pl.when(g == DSTEP)
            def _():
                for step in range(1, NZ):
                    z_copy(step).wait()
                dt[core * 16 + node] = jnp.concatenate([dz[i] for i in range(NZ)], axis=1)
                for k in range(1, 4):
                    d_copy(0, k).start()

            @pl.when(g == DSTEP + DHOP)
            def _():
                for k in range(1, 4):
                    d_copy(0, k).wait()
                for k in range(1, 4):
                    d_copy(1, k).start()

            @pl.when(g == DSTEP + 2 * DHOP)
            def _():
                for k in range(1, 4):
                    d_copy(1, k).wait()
                d_copy(2).start()

            @pl.when(g == INVERT)
            def _():
                d_copy(2).wait()
                for block in range(32):
                    dtf[pl.ds(block_column(block) * 16, 16), :] = dt[block].astype(F32)
                packed = dtf[...].T
                row = lax.broadcasted_iota(jnp.int32, (NB, NB), 0)
                column = lax.broadcasted_iota(jnp.int32, (NB, NB), 1)
                uinv[...] = jnp.where(column >= row, packed, 0.0).astype(BF16)
                linv[...] = jnp.where(column < row, packed, jnp.where(column == row, 1.0, 0.0)).astype(BF16)

        @pl.when(g == early)
        def _():
            solve_u(order[0])
            solve_u(order[1])

        part = g - solve

        @pl.when((part >= 0) & (part < ITEMS))
        def _():
            block, item = lax.div(part, 3), lax.rem(part, 3)

            @pl.when(item == 0)
            def _():
                first = pl.multiple_of(block * BLK, BLK)
                rows = pl.ds(first, BLK)
                l = jnp.dot(lraw[rows, :], uinv[...], preferred_element_type=F32).astype(BF16)
                lsol[rows, :] = l

                @pl.when(source)
                def _():
                    for t in range(4):
                        store(first, 2 * t, -l[:, t * 128:(t + 1) * 128].astype(F32))

            @pl.when(item != 0)
            def _():
                update_block(jnp.where(item == 1, order[0], order[1]), block)

        @pl.when((g >= late) & (g < late + ROWS // BLK // PER))
        def _():
            @pl.when(g == late)
            def _():
                solve_u(order[2])

            for i in range(PER):
                update_block(order[2], (g - late) * PER + i)

        return carry

    lax.fori_loop(0, TOTAL, step_body, 0)

    solve_u(order[3])

    def last_body(b, carry):
        update_block(order[3], b)
        return carry

    lax.fori_loop(0, ROWS // BLK, last_body, 0)

    @pl.when(z == 0)
    def _():
        for t in range(4):
            s_low[pl.ds(2 * t, NB, stride=8), :] = jnp.where(source, 0.0, -ub[t, :, 0:128].astype(F32))
            s_low[pl.ds(2 * t + 1, NB, stride=8), :] = -ub[t, :, 128:256].astype(F32)

    for last in range(SLOTS):
        for way, hop in ways:
            @pl.when(hop != NZ - 1)
            def _():
                u_copy(way, last).wait_send()

        for k in range(2):
            for dim in range(4):
                @pl.when(sends[k][dim])
                def _():
                    l_copy(own[k], last, nears[dim], l_send.at[k, dim]).wait_send()

            @pl.when(to_sibling)
            def _():
                l_copy(own[k], last, sibling, s_send.at[k]).wait_send()

            @pl.when(source)
            def _():
                l_copy(others[k], last, sibling, s_send.at[2 + k]).wait_send()


def settle(s_low, s_high, a_ref, out_ref, buf, sem):
    z = lax.axis_index("prow")
    source = lax.axis_index("pcol") == 0
    even = lax.broadcasted_iota(jnp.int32, (8, 128), 0) % 2 == 0
    size = OUT * 8

    def copy(b):
        rows = pl.ds(pl.multiple_of(b * size, size), size)
        return pltpu.make_async_copy(buf.at[rows], out_ref.at[rows], sem.at[b])

    def body(s_ref, first, b, carry):
        head = (z == 0) & (b < NB // OUT)
        keep_even = jnp.where(head == source, 1.0, 0.0)
        keep_odd = jnp.where(head, 0.0, 1.0)
        keep = jnp.where(even, keep_even, keep_odd)
        rows = pl.ds(pl.multiple_of(b * size, size), size)
        a = a_ref[rows, :].astype(F32).reshape(OUT, 8, 128) * keep[None]
        part = pl.ds(pl.multiple_of((b - first) * size, size), size)
        buf[rows, :] = (a.reshape(size, 128) - s_ref[part, :]).astype(BF16)
        copy(b).start()
        return carry

    def finish(b, carry):
        copy(b).wait()
        return carry

    half = ROWS // OUT // 2
    lax.fori_loop(0, half, functools.partial(body, s_low, 0), 0)
    lax.fori_loop(half, 2 * half, functools.partial(body, s_high, half), 0)
    lax.fori_loop(0, ROWS // OUT, finish, 0)


def shards(matrix, diag_inverses):
    flat = matrix.reshape(ROWS, 2, 4, 128).transpose(0, 2, 1, 3).reshape(ROWS * 8, 128)
    dma = pltpu.SemaphoreType.DMA
    vmem = pl.BlockSpec(memory_space=pltpu.VMEM)
    low, high, a = pl.pallas_call(
        kernel,
        out_shape=[
            jax.ShapeDtypeStruct((ROWS * 4, 128), F32),
            jax.ShapeDtypeStruct((ROWS * 4, 128), F32),
            jax.ShapeDtypeStruct((ROWS * 8, 128), BF16),
        ],
        in_specs=[pl.BlockSpec(memory_space=pltpu.HBM), vmem],
        out_specs=[vmem] * 3,
        scratch_shapes=[
            pltpu.VMEM((4 * LCH * 8, 128), F32),
            pltpu.VMEM((ROWS, NB), BF16),
            pltpu.VMEM((ROWS, NB), BF16),
            pltpu.VMEM((4, NB, 256), BF16),
            pltpu.VMEM((4, NB, 256), BF16),
            pltpu.VMEM((NB, NB), BF16),
            pltpu.VMEM((NB, NB), BF16),
            pltpu.VMEM((NZ, 16, 64), BF16),
            pltpu.VMEM((32, 16, NB), BF16),
            pltpu.VMEM((NB, NB), F32),
            dma((6,)),
            dma((2, 4, SLOTS)),
            dma((4, LSTEPS)),
            dma((4, SLOTS)),
            dma((2, SLOTS)),
            dma((2, STEPS)),
            dma((NZ - 1,)),
            dma((NZ - 1,)),
            dma((3, 4)),
            dma((3, 4)),
        ],
        compiler_params=pltpu.CompilerParams(
            collective_id=0, has_side_effects=True, vmem_limit_bytes=33 * 2**20),
    )(flat, diag_inverses.T)
    out = pl.pallas_call(
        settle,
        out_shape=jax.ShapeDtypeStruct((ROWS * 8, 128), BF16),
        in_specs=[vmem] * 3,
        out_specs=pl.BlockSpec(memory_space=pl.ANY),
        scratch_shapes=[pltpu.VMEM((ROWS * 8, 128), BF16), dma((ROWS // OUT,))],
        compiler_params=pltpu.CompilerParams(vmem_limit_bytes=12 * 2**20),
    )(low, high, a)
    return out.reshape(ROWS, 4, 2, 128).transpose(0, 2, 1, 3).reshape(matrix.shape)


def solution(mesh):
    in_specs = (P(None, "prow", None, "pcol"), P("prow", "pcol"))
    out_specs = P(None, "prow", None, "pcol")
    return jax.shard_map(shards, mesh=mesh, in_specs=in_specs, out_specs=out_specs, check_vma=False)
```

time: 73.2 us -> 56.1 us (0.77)
  Pallas kernels: 69.6 us -> 54.7 us
  local copies, waits for them, and re-layouts: 3.47 us -> 0.69 us
    pallas_call x1, Pallas kernels: 66.7 us -> 51.8 us  [shards(): pl.pallas_call(kernel, out_shape=[jax.ShapeDtypeStruct((ROWS * 4, 128), F...]
    unnamed x4 -> x2, local copies, waits for them, and re-layouts: 3.47 us -> 0.69 us
where the time goes in v4:
time: 56.1 us; the launch traced here: 55.4 us
  Pallas kernels  54.7 us (98%)
  local copies, waits for them, and re-layouts  0.69 us (1%)
    pallas_call x1, Pallas kernels, shards(): pl.pallas_call(kernel, out_shape=[jax.ShapeDtypeStruct((ROWS * 4, 128), F...  51.8 us
    pallas_call x1, Pallas kernels, shards(): pl.pallas_call(settle, out_shape=jax.ShapeDtypeStruct((ROWS * 8, 128), BF...  2.88 us

profile of v4, /device:TPU:96, one launch (start us, length us, event | category | flops | bytes accessed | tf_op | source)
XLA Modules:
  0.0 55.4 jit_solution(2018513460823849599)
XLA Ops:
  0.0 0.0 copy-start
  0.0 0.7 %copy-done = bf16[64,16]{0,1:T(8,128)(2,1)S(1)} copy-done((bf16[64,16]{0,1:T(8,128)(2,1)S(1)}, bf16[64,16]{0,1:T(8,128)(2,1)}, u32[]{:S(2)}) %copy-start) | copy-done | bytes 2072
  0.7 51.8 %shard_map.28 = (f32[12288,128]{1,0:T(8,128)S(1)}, f32[12288,128]{1,0:T(8,128)S(1)}, bf16[24576,128]{1,0:T(8,128)(2,1)S(1)}) custom-call(bf16[24576,128]{1,0:T(8,128)(2,1)} %bitcast.12, bf16[16,64]{1,0:T(8,128)(2,1)S(1)} %bitcast.11), custom_call_target="tpu_custom_call" | custom-call | tf_op jit(solution)/shard_map/pallas_call | solution.py:407
  52.5 2.9 %shard_map.29 = bf16[24576,128]{1,0:T(8,128)(2,1)} custom-call(f32[12288,128]{1,0:T(8,128)S(1)} %get-tuple-element.8.s_low, f32[12288,128]{1,0:T(8,128)S(1)} %get-tuple-element.9.s_high, bf16[24576,128]{1,0:T(8,128)(2,1)S(1)} %get-tuple-element.10.a_ref), custom_call_target="tpu_custom_call" | custom-call | tf_op jit(solution)/shard_map/pallas_call | solution.py:441
Async XLA Ops:
  0.0 0.7 %copy-start = (bf16[64,16]{0,1:T(8,128)(2,1)S(1)}, bf16[64,16]{0,1:T(8,128)(2,1)}, u32[]{:S(2)}) copy-start(bf16[64,16]{0,1:T(8,128)(2,1)} %param.3) | copy-start | bytes 6148

commit v5 on v4

--- a/solution.py
+++ b/solution.py
@@ -18,7 +18,7 @@
 UCH = 2 * NB // STEPS
 UPER = NB // UCH
 BLK = 512
-UHOP, LHOP, CHOP = 6, 6, 3
+UHOP, LHOP, CHOP = 5, 5, 2
 SLOTS = 4
 TOTAL = STEPS + (NZ - 1) * UHOP
 DSTEP, DHOP = 6, 6
@@ -161,8 +161,9 @@
     far_t = 2 - near_t
     order = [near_t, jnp.where(middle, 2, near_t + 1), jnp.where(middle, 1, far_t), far_t + 1]
 
-    def solve_u(t):
-        ub[t] = jnp.dot(linv[...], uraw[t], preferred_element_type=F32).astype(BF16)
+    def solve_u(slot):
+        u = jnp.dot(linv[...], uraw[order[slot]], preferred_element_type=F32).astype(BF16)
+        ub[slot // 2, :, slot % 2 * 256:slot % 2 * 256 + 256] = u
 
     def store(first, offset, value):
         for half, ref in enumerate((s_low, s_high)):
@@ -170,18 +171,19 @@
             def _():
                 ref[pl.ds((first - half * (ROWS // 2)) * 8 + offset, BLK, stride=8), :] = value
 
-    def update(t, first, l):
-        p = jnp.dot(l, ub[t], preferred_element_type=F32)
+    def update(b, slots):
+        first = pl.multiple_of(b * BLK, BLK)
+        low = slots[0] % 2 * 256
+        u = ub[slots[0] // 2, :, low:low + 256 * len(slots)]
+        p = jnp.dot(lsol[pl.ds(first, BLK), :], u, preferred_element_type=F32)
 
         @pl.when(plain)
         def _():
-            store(first, 2 * t, p[:, 0:128])
-
-        store(first, 2 * t + 1, p[:, 128:256])
-
-    def update_block(t, b):
-        first = pl.multiple_of(b * BLK, BLK)
-        update(t, first, lsol[pl.ds(first, BLK), :])
+            for i, slot in enumerate(slots):
+                store(first, 2 * order[slot], p[:, i * 256:i * 256 + 128])
+
+        for i, slot in enumerate(slots):
+            store(first, 2 * order[slot] + 1, p[:, i * 256 + 128:i * 256 + 256])
 
     load_a(0).wait()
 
@@ -295,8 +297,8 @@
 
         @pl.when(g == early)
         def _():
-            solve_u(order[0])
-            solve_u(order[1])
+            solve_u(0)
+            solve_u(1)
 
         part = g - solve
 
@@ -316,36 +318,45 @@
                     for t in range(4):
                         store(first, 2 * t, -l[:, t * 128:(t + 1) * 128].astype(F32))
 
-            @pl.when(item != 0)
-            def _():
-                update_block(jnp.where(item == 1, order[0], order[1]), block)
+            for slot in range(2):
+                @pl.when(item == slot + 1)
+                def _():
+                    update(block, (slot,))
 
         @pl.when((g >= late) & (g < late + ROWS // BLK // PER))
         def _():
             @pl.when(g == late)
             def _():
-                solve_u(order[2])
+                solve_u(2)
 
             for i in range(PER):
-                update_block(order[2], (g - late) * PER + i)
+                update((g - late) * PER + i, (2,))
 
         return carry
 
     lax.fori_loop(0, TOTAL, step_body, 0)
 
-    solve_u(order[3])
-
-    def last_body(b, carry):
-        update_block(order[3], b)
-        return carry
-
-    lax.fori_loop(0, ROWS // BLK, last_body, 0)
+    solve_u(3)
+
+    last_t = order[3]
+    for b in range(ROWS // BLK):
+        ref, first = (s_low, b * BLK) if b < ROWS // BLK // 2 else (s_high, b * BLK - ROWS // 2)
+        p = jnp.dot(lsol[b * BLK:(b + 1) * BLK, :], ub[1, :, 256:512], preferred_element_type=F32)
+        for j in range(2):
+            ref[pl.ds(first * 8 + 2 * last_t + j, BLK, stride=8), :] = p[:, j * 128:(j + 1) * 128]
+
+    @pl.when(source)
+    def _():
+        lanes = pl.ds(pl.multiple_of(last_t * 128, 128), 128)
+        for half, ref in enumerate((s_low, s_high)):
+            l = lsol[pl.ds(half * (ROWS // 2), ROWS // 2), lanes].astype(F32)
+            ref[pl.ds(2 * last_t, ROWS // 2, stride=8), :] = -l
 
     @pl.when(z == 0)
     def _():
         for t in range(4):
-            s_low[pl.ds(2 * t, NB, stride=8), :] = jnp.where(source, 0.0, -ub[t, :, 0:128].astype(F32))
-            s_low[pl.ds(2 * t + 1, NB, stride=8), :] = -ub[t, :, 128:256].astype(F32)
+            s_low[pl.ds(2 * t, NB, stride=8), :] = jnp.where(source, 0.0, -ub[t // 2, :, t % 2 * 256:t % 2 * 256 + 128].astype(F32))
+            s_low[pl.ds(2 * t + 1, NB, stride=8), :] = -ub[t // 2, :, t % 2 * 256 + 128:t % 2 * 256 + 256].astype(F32)
 
     for last in range(SLOTS):
         for way, hop in ways:
@@ -418,7 +429,7 @@
             pltpu.VMEM((ROWS, NB), BF16),
             pltpu.VMEM((ROWS, NB), BF16),
             pltpu.VMEM((4, NB, 256), BF16),
-            pltpu.VMEM((4, NB, 256), BF16),
+            pltpu.VMEM((2, NB, NB), BF16),
             pltpu.VMEM((NB, NB), BF16),
             pltpu.VMEM((NB, NB), BF16),
             pltpu.VMEM((NZ, 16, 64), BF16),

time: 56.1 us -> 53.7 us (0.957); the launches traced: 55.4 us -> 53.6 us
  Pallas kernels: 54.7 us -> 52.9 us
    pallas_call x1, Pallas kernels: 51.8 us -> 50.1 us  [shards(): pl.pallas_call(kernel, out_shape=[jax.ShapeDtypeStruct((ROWS * 4, 128), F...]
where the time goes in v5:
time: 53.7 us; the launch traced here: 53.6 us
  Pallas kernels  52.9 us (99%)
  local copies, waits for them, and re-layouts  0.69 us (1%)
    pallas_call x1, Pallas kernels, shards(): pl.pallas_call(kernel, out_shape=[jax.ShapeDtypeStruct((ROWS * 4, 128), F...  50.1 us
    pallas_call x1, Pallas kernels, shards(): pl.pallas_call(settle, out_shape=jax.ShapeDtypeStruct((ROWS * 8, 128), BF...  2.88 us

profile of v5, /device:TPU:96, one launch (start us, length us, event | category | flops | bytes accessed | tf_op | source)
XLA Modules:
  0.0 53.6 jit_solution(17588875294747670118)
XLA Ops:
  0.0 0.0 copy-start
  0.0 0.7 %copy-done = bf16[64,16]{0,1:T(8,128)(2,1)S(1)} copy-done((bf16[64,16]{0,1:T(8,128)(2,1)S(1)}, bf16[64,16]{0,1:T(8,128)(2,1)}, u32[]{:S(2)}) %copy-start) | copy-done | bytes 2072
  0.7 50.1 %shard_map.28 = (f32[12288,128]{1,0:T(8,128)S(1)}, f32[12288,128]{1,0:T(8,128)S(1)}, bf16[24576,128]{1,0:T(8,128)(2,1)S(1)}) custom-call(bf16[24576,128]{1,0:T(8,128)(2,1)} %bitcast.12, bf16[16,64]{1,0:T(8,128)(2,1)S(1)} %bitcast.11), custom_call_target="tpu_custom_call" | custom-call | tf_op jit(solution)/shard_map/pallas_call | solution.py:418
  50.8 2.9 %shard_map.29 = bf16[24576,128]{1,0:T(8,128)(2,1)} custom-call(f32[12288,128]{1,0:T(8,128)S(1)} %get-tuple-element.8.s_low, f32[12288,128]{1,0:T(8,128)S(1)} %get-tuple-element.9.s_high, bf16[24576,128]{1,0:T(8,128)(2,1)S(1)} %get-tuple-element.10.a_ref), custom_call_target="tpu_custom_call" | custom-call | tf_op jit(solution)/shard_map/pallas_call | solution.py:452
Async XLA Ops:
  0.0 0.7 %copy-start = (bf16[64,16]{0,1:T(8,128)(2,1)S(1)}, bf16[64,16]{0,1:T(8,128)(2,1)}, u32[]{:S(2)}) copy-start(bf16[64,16]{0,1:T(8,128)(2,1)} %param.3) | copy-start | bytes 6148

commit v6 on v5

--- a/solution.py
+++ b/solution.py
@@ -18,14 +18,13 @@
 UCH = 2 * NB // STEPS
 UPER = NB // UCH
 BLK = 512
-UHOP, LHOP, CHOP = 5, 5, 2
+UHOP, LHOP, CHOP = 4, 4, 2
 SLOTS = 4
-TOTAL = STEPS + (NZ - 1) * UHOP
+TOTAL = max(STEPS + (NZ - 1) * UHOP, STEPS + NZ // 2 * UHOP + 3 * ROWS // NB)
 DSTEP, DHOP = 6, 6
 INVERT = DSTEP + 2 * DHOP + 3
 OUT = 256
 ITEMS = 3 * (ROWS // BLK)
-PER = 3
 
 
 def parent(tree, node):
@@ -185,6 +184,15 @@
         for i, slot in enumerate(slots):
             store(first, 2 * order[slot] + 1, p[:, i * 256 + 128:i * 256 + 256])
 
+    def quarter(slot):
+        low = slot % 2 * 256
+        for b in range(ROWS // BLK):
+            ref, first = (s_low, b * BLK) if b < ROWS // BLK // 2 else (s_high, b * BLK - ROWS // 2)
+            u = ub[slot // 2, :, low:low + 256]
+            p = jnp.dot(lsol[b * BLK:(b + 1) * BLK, :], u, preferred_element_type=F32)
+            for j in range(2):
+                ref[pl.ds(first * 8 + 2 * order[slot] + j, BLK, stride=8), :] = p[:, j * 128:(j + 1) * 128]
+
     load_a(0).wait()
 
     def step_body(g, carry):
@@ -323,14 +331,10 @@
                 def _():
                     update(block, (slot,))
 
-        @pl.when((g >= late) & (g < late + ROWS // BLK // PER))
-        def _():
-            @pl.when(g == late)
-            def _():
-                solve_u(2)
-
-            for i in range(PER):
-                update((g - late) * PER + i, (2,))
+        @pl.when(g == late)
+        def _():
+            solve_u(2)
+            quarter(2)
 
         return carry
 
@@ -338,19 +342,16 @@
 
     solve_u(3)
 
-    last_t = order[3]
-    for b in range(ROWS // BLK):
-        ref, first = (s_low, b * BLK) if b < ROWS // BLK // 2 else (s_high, b * BLK - ROWS // 2)
-        p = jnp.dot(lsol[b * BLK:(b + 1) * BLK, :], ub[1, :, 256:512], preferred_element_type=F32)
-        for j in range(2):
-            ref[pl.ds(first * 8 + 2 * last_t + j, BLK, stride=8), :] = p[:, j * 128:(j + 1) * 128]
+    quarter(3)
 
     @pl.when(source)
     def _():
-        lanes = pl.ds(pl.multiple_of(last_t * 128, 128), 128)
-        for half, ref in enumerate((s_low, s_high)):
-            l = lsol[pl.ds(half * (ROWS // 2), ROWS // 2), lanes].astype(F32)
-            ref[pl.ds(2 * last_t, ROWS // 2, stride=8), :] = -l
+        for slot in (2, 3):
+            t = order[slot]
+            lanes = pl.ds(pl.multiple_of(t * 128, 128), 128)
+            for half, ref in enumerate((s_low, s_high)):
+                l = lsol[pl.ds(half * (ROWS // 2), ROWS // 2), lanes].astype(F32)
+                ref[pl.ds(2 * t, ROWS // 2, stride=8), :] = -l
 
     @pl.when(z == 0)
     def _():

time: 53.7 us -> 52.1 us (0.970)
  Pallas kernels: 52.9 us -> 51.2 us
    pallas_call x1, Pallas kernels: 50.1 us -> 48.3 us  [shards(): pl.pallas_call(kernel, out_shape=[jax.ShapeDtypeStruct((ROWS * 4, 128), F...]
where the time goes in v6:
time: 52.1 us; the launch traced here: 51.9 us
  Pallas kernels  51.2 us (98%)
  local copies, waits for them, and re-layouts  0.69 us (1%)
    pallas_call x1, Pallas kernels, shards(): pl.pallas_call(kernel, out_shape=[jax.ShapeDtypeStruct((ROWS * 4, 128), F...  48.3 us
    pallas_call x1, Pallas kernels, shards(): pl.pallas_call(settle, out_shape=jax.ShapeDtypeStruct((ROWS * 8, 128), BF...  2.88 us

profile of v6, /device:TPU:96, one launch (start us, length us, event | category | flops | bytes accessed | tf_op | source)
XLA Modules:
  0.0 51.9 jit_solution(11603305258304797146)
XLA Ops:
  0.0 0.0 copy-start
  0.0 0.7 %copy-done = bf16[64,16]{0,1:T(8,128)(2,1)S(1)} copy-done((bf16[64,16]{0,1:T(8,128)(2,1)S(1)}, bf16[64,16]{0,1:T(8,128)(2,1)}, u32[]{:S(2)}) %copy-start) | copy-done | bytes 2072
  0.7 48.3 %shard_map.28 = (f32[12288,128]{1,0:T(8,128)S(1)}, f32[12288,128]{1,0:T(8,128)S(1)}, bf16[24576,128]{1,0:T(8,128)(2,1)S(1)}) custom-call(bf16[24576,128]{1,0:T(8,128)(2,1)} %bitcast.12, bf16[16,64]{1,0:T(8,128)(2,1)S(1)} %bitcast.11), custom_call_target="tpu_custom_call" | custom-call | tf_op jit(solution)/shard_map/pallas_call | solution.py:419
  49.0 2.9 %shard_map.29 = bf16[24576,128]{1,0:T(8,128)(2,1)} custom-call(f32[12288,128]{1,0:T(8,128)S(1)} %get-tuple-element.8.s_low, f32[12288,128]{1,0:T(8,128)S(1)} %get-tuple-element.9.s_high, bf16[24576,128]{1,0:T(8,128)(2,1)S(1)} %get-tuple-element.10.a_ref), custom_call_target="tpu_custom_call" | custom-call | tf_op jit(solution)/shard_map/pallas_call | solution.py:453
Async XLA Ops:
  0.0 0.7 %copy-start = (bf16[64,16]{0,1:T(8,128)(2,1)S(1)}, bf16[64,16]{0,1:T(8,128)(2,1)}, u32[]{:S(2)}) copy-start(bf16[64,16]{0,1:T(8,128)(2,1)} %param.3) | copy-start | bytes 6148
